TPU v7x, 32 devices: a whole 2x2x4 slice. The times are simulated.
32 devices in a mesh: gx: 4 (over y, x), gy: 4 (over z), gz: 2 (over core).
Axes of the slice: x: 2, y: 2, z: 4, core: 2. Of those that a mesh axis runs over, the one named last changes fastest.
Arguments:
- well_sources: float32 [1536, 64], P(('gx', 'gy'), 'gz'), may hold values from -6 to 6
- well_owner: int32 [1536, 1], P(('gx', 'gy')), may hold values from 0 to 15; in each aligned block of 96 rows (0 to 95, 96 to 191, ...) at most 12 rows name the same one
- well_cell: int32 [1536], P(('gx', 'gy')), may hold values from 0 to 2047
- flow_sign: int32 [3, 64, 64, 512], P(None, 'gz', 'gx', 'gy'), may hold values from 0 to 7
- courant: float32 [3, 64, 64, 512], P(None, 'gz', 'gx', 'gy'), may hold values from 0.01 to 0.3
- tracer: float32 [3, 64, 64, 512], P(None, 'gz', 'gx', 'gy'), may hold values from -6 to 6
Outputs:
- lambda_start: float32 [64, 64, 512], P('gz', 'gx', 'gy')
- smoothed: float32 [512, 64, 64], P(('gx', 'gy', 'gz'))
Inputs may be any that keep to these rules, and one draw needn't show every extreme that they name: `well_owner`: among the wells of one index of gx+gy at most 12 name the same owner, a bound that some block of them reaches.
All inputs are finite; a program needn't handle non-finite values.
Results may differ from a plain program's by a relative error of at most 0.00015.
Values sent between devices are 32-bit elements; how exact they have to be, the bound alone decides.
A program may use at most 128 MiB of HBM per device.

v0:
```python
import math

import jax
import jax.numpy as jnp
from jax import lax
from jax.sharding import PartitionSpec as P

STEPS = 3


def with_halo(block, sides, width):
    for axis, dim in sides:
        count = lax.axis_size(axis)
        forward = [(i, i + 1) for i in range(count - 1)]
        backward = [(target, source) for source, target in forward]
        low = lax.ppermute(
            lax.slice_in_dim(block, block.shape[dim] - width, None, axis=dim), axis, forward
        )
        high = lax.ppermute(lax.slice_in_dim(block, 0, width, axis=dim), axis, backward)
        block = jnp.concatenate([low, block, high], axis=dim)
    return block


def correlation(extent, length):
    places = jnp.arange(extent).astype(jnp.float32)
    spacing = jnp.abs(places[:, None] - places[None, :])
    return jnp.exp(-spacing / length) / math.sqrt(length)


def advance_weights(adjoint, rising_pad, falling_pad, staying):
    padded = with_halo(adjoint, (("gx", 1), ("gy", 2), ("gz", 0)), 1)
    updated = staying * adjoint
    updated = (
        updated
        + rising_pad[0, 1:-1, 2:, 1:-1] * padded[1:-1, 2:, 1:-1]
        + falling_pad[0, 1:-1, :-2, 1:-1] * padded[1:-1, :-2, 1:-1]
    )
    updated = (
        updated
        + rising_pad[1, 1:-1, 1:-1, 2:] * padded[1:-1, 1:-1, 2:]
        + falling_pad[1, 1:-1, 1:-1, :-2] * padded[1:-1, 1:-1, :-2]
    )
    updated = (
        updated
        + rising_pad[2, 2:, 1:-1, 1:-1] * padded[2:, 1:-1, 1:-1]
        + falling_pad[2, :-2, 1:-1, 1:-1] * padded[:-2, 1:-1, 1:-1]
    )
    return updated


def per_device(well_sources, well_owner, well_cell, flow_sign, courant, tracer):
    brick_z, brick_x, brick_y = (courant.shape[1], courant.shape[2], courant.shape[3])
    columns = brick_x * brick_y
    groups = lax.axis_size("gx") * lax.axis_size("gy")
    my_owner = lax.axis_index("gx") * lax.axis_size("gy") + lax.axis_index("gy")
    owners = well_owner[:, 0]
    all_sources, all_owner, all_cell = (
        lax.all_gather(well_sources, ("gx", "gy"), axis=0, tiled=True),
        lax.all_gather(owners, ("gx", "gy"), axis=0, tiled=True),
        lax.all_gather(well_cell, ("gx", "gy"), axis=0, tiled=True),
    )
    target = jnp.where(all_owner == my_owner, all_cell, columns)
    landed = (
        jnp.zeros((brick_z, columns), jnp.float32)
        .at[:, target]
        .add(jnp.transpose(all_sources), mode="drop")
    )
    adjoint = landed.reshape(brick_z, brick_x, brick_y)
    upward = jnp.stack([flow_sign // 1 % 2, flow_sign // 2 % 2, flow_sign // 4 % 2], axis=1).astype(
        jnp.float32
    )
    staying = 1.0 - (courant[0] + courant[1] + courant[2])
    gradient = jnp.zeros((brick_z, brick_x, brick_y), jnp.float32)
    weights = jnp.stack([courant[None] * upward, courant[None] * (1.0 - upward)])
    weight_pad = with_halo(weights, (("gx", 4), ("gy", 5), ("gz", 3)), 1)
    for step in reversed(range(STEPS)):
        adjoint = advance_weights(adjoint, weight_pad[0, step], weight_pad[1, step], staying)
        gradient = gradient + adjoint * tracer[step]
    highest = lax.Precision.HIGHEST
    y_lines = lax.all_to_all(gradient, "gy", split_axis=1, concat_axis=2, tiled=True)
    x_share = y_lines.shape[1]
    full_y = y_lines.shape[2]
    line_count = y_lines.shape[0] * x_share
    smooth_y = lax.dot_general(
        correlation(full_y, 2 * brick_y),
        y_lines.reshape(line_count, full_y),
        (((1,), (1,)), ((), ())),
        precision=highest,
        preferred_element_type=jnp.float32,
    )
    planes = lax.all_to_all(
        lax.all_to_all(smooth_y, ("gx", "gy"), split_axis=0, concat_axis=1, tiled=True),
        "gz",
        split_axis=0,
        concat_axis=1,
        tiled=True,
    )
    y_rows = planes.shape[0]
    depth_groups = lax.axis_size("gz")
    plane_view = planes.reshape(y_rows, depth_groups, groups, brick_z, x_share)
    full_x = groups * x_share
    table_x = correlation(full_x, 2 * brick_x).reshape(full_x, groups, x_share)
    smooth_x = jnp.einsum("ykdza,jda->ykzj", plane_view, table_x, precision=highest)
    full_z = depth_groups * brick_z
    smooth_x = smooth_x.reshape(y_rows, full_z, full_x)
    smoothed = jnp.einsum(
        "yzj,iz->yij", smooth_x, correlation(full_z, 2 * brick_z), precision=highest
    )
    return (adjoint, smoothed)


def solution(mesh):
    return jax.shard_map(
        per_device,
        mesh=mesh,
        in_specs=(
            P(("gx", "gy"), "gz"),
            P(("gx", "gy"), None),
            P(("gx", "gy")),
            P(None, "gz", "gx", "gy"),
            P(None, "gz", "gx", "gy"),
            P(None, "gz", "gx", "gy"),
        ),
        out_specs=(P("gz", "gx", "gy"), P(("gx", "gy", "gz"), None, None)),
        check_vma=False,
    )
```

profile of v0, /device:TPU:0, one launch (start us, length us, event | category | flops | bytes accessed | tf_op | source)
XLA Modules:
  0.0 339.9 jit_solution(12330192928112615398)
XLA Ops:
  0.6 2.8 fusion.8
  6.1 5.6 %collective-permute-start = (f32[2,3,3,32,1,128]{5,3,4,2,1,0:T(8,128)}, f32[2,3,3,32,1,128]{5,3,4,2,1,0:T(8,128)}, u32[]{:S(2)}, u32[]{:S(2)}) collective-permute-start(f32[2,3,3,32,1,128]{5,3,4,2,1,0:T(8,128)} %get-tuple-element.22), channel_id=1, source_target_pairs={{0,8},{8,16},{16,24},{1,9},{9,17},{17,25},{2,10},{10,18},{18,26},{... | collective-permute-start | bytes 884744 | tf_op jit(solution)/shard_map/ppermute | solution.py:16
  14.7 78.5 %all-reduce.2 = (s32[1536]{0:T(1024)S(1)}, s32[1536]{0:T(1024)S(1)}) all-reduce(s32[1536]{0:T(1024)S(1)} %dynamic-update-slice.1, s32[1536]{0:T(1024)S(1)} %bitcast_dynamic-update-slice_fusion), channel_id=1, replica_groups=mesh['gx'=4,'gy'=4,'gz'=2] {'gx','gy'}, use_global_device_ids=true, to_apply=%add.1 | all-reduce | flops 3072 | bytes 24576
  93.2 37.5 %all-gather.1 = f32[16,96,32]{1,2,0:T(8,128)S(1)} all-gather(f32[1,96,32]{1,2,0:T(8,128)S(1)} %bitcast.161), channel_id=1, replica_groups=mesh['gx'=4,'gy'=4,'gz'=2] {'gx','gy'}, dimensions={0}, use_global_device_ids=true | all-gather | bytes 208896 | tf_op jit(solution)/shard_map/all_gather | solution.py:58
  131.9 10.1 %scatter_custom_fusion = f32[32,2048]{0,1:T(8,128)} fusion(s32[1536]{0:T(1024)S(1)} %compare_select_fusion, f32[1536,32]{1,0:T(8,128)} %bitcast.160, f32[]{:T(128)} %constant.78.clone.1), kind=kCustom, calls=%fused_computation.47 | custom fusion | flops 49152 | bytes 262656 | tf_op jit(solution)/shard_map/scatter-add | solution.py:66
  142.0 1.5 copy.62
  143.6 1.3 collective-permute-start.6
  144.9 4.5 %collective-permute-start.7 = (f32[32,1,128]{2,0,1:T(8,128)S(1)}, f32[32,1,128]{2,0,1:T(8,128)S(1)}, u32[]{:S(2)}, u32[]{:S(2)}) collective-permute-start(f32[32,1,128]{2,0,1:T(8,128)S(1)} %get-tuple-element.48), channel_id=1, source_target_pairs={{0,8},{8,16},{16,24},{1,9},{9,17},{17,25},{2,10},{10,18},{18,26},{... | collective-permute-start | bytes 49160 | tf_op jit(solution)/shard_map/ppermute | solution.py:16
  149.4 2.6 pad_maximum_fusion.1
  152.1 6.2 %fusion.95 = (f32[2,3,3,32,18,1]{5,3,4,2,1,0:T(8,128)}, f32[2,3,3,32,18,1]{5,3,4,2,1,0:T(8,128)}) fusion(f32[2,3,3,32,18,128]{5,3,4,2,1,0:T(8,128)S(1)} %pad_maximum_fusion.1), kind=kLoop, calls=%fused_computation.231 | loop fusion | bytes 165888 | tf_op jit(solution)/shard_map/slice | solution.py:17
  158.3 4.4 %copy.70 = f32[2,3,3,32,18,1]{3,0,5,4,2,1:T(2,128)} copy(f32[2,3,3,32,18,1]{5,3,4,2,1,0:T(8,128)} %get-tuple-element.20) | data formatting | bytes 82944 | tf_op jit(solution)/shard_map/slice | solution.py:17
  162.7 4.5 %collective-permute-start.2 = (f32[2,3,3,32,18,1]{3,0,5,4,2,1:T(2,128)}, f32[2,3,3,32,18,1]{3,0,5,4,2,1:T(2,128)}, u32[]{:S(2)}, u32[]{:S(2)}) collective-permute-start(f32[2,3,3,32,18,1]{3,0,5,4,2,1:T(2,128)} %copy.70), channel_id=1, source_target_pairs={{0,2},{2,4},{4,6},{1,3},{3,5},{5,7},{8,10},{10,12},{12,14},{9,11},... | collective-permute-start | bytes 124424 | tf_op jit(solution)/shard_map/ppermute | solution.py:16
  167.2 4.4 %copy.71 = f32[2,3,3,32,18,1]{3,0,5,4,2,1:T(2,128)} copy(f32[2,3,3,32,18,1]{5,3,4,2,1,0:T(8,128)} %get-tuple-element.21) | data formatting | bytes 82944 | tf_op jit(solution)/shard_map/slice | solution.py:19
  171.6 1.5 collective-permute-start.3
  173.9 4.5 %copy.72 = f32[2,3,3,32,18,1]{5,3,4,2,1,0:T(8,128)} copy(f32[2,3,3,32,18,1]{3,0,5,4,2,1:T(2,128)} %collective-permute-done.2) | data formatting | bytes 82944 | tf_op jit(solution)/shard_map/ppermute | solution.py:16
  179.2 4.5 %copy.73 = f32[2,3,3,32,18,1]{5,3,4,2,1,0:T(8,128)} copy(f32[2,3,3,32,18,1]{3,0,5,4,2,1:T(2,128)} %collective-permute-done.3) | data formatting | bytes 82944 | tf_op jit(solution)/shard_map/ppermute | solution.py:19
  183.7 6.6 %pad_maximum_fusion.7 = (f32[2,3,3,1,18,130]{5,3,4,2,1,0:T(1,128)S(1)}, f32[2,3,3,1,18,130]{5,3,4,2,1,0:T(1,128)S(1)}) fusion(f32[2,3,3,32,18,1]{5,3,4,2,1,0:T(8,128)} %copy.73, f32[2,3,3,32,18,1]{5,3,4,2,1,0:T(8,128)} %copy.72, f32[2,3,3,32,1,128]{5,3,4,2,1,0:T(8,128)} %collective-permute-done.1, f32[2,3,3,32,1,128]{5,3,4,2,1,0:T(8,128)} %collective-permute-done, ...), kind=kLoop, calls=%fused_computation.55 | loop fusion | flops 421200 | bytes 5728320 | tf_op jit(solution)/shard_map/slice | solution.py:17
  190.3 1.3 collective-permute-start.4
  191.6 1.3 collective-permute-start.5
  193.0 1.3 collective-permute-start.8
  194.3 4.6 %collective-permute-start.9 = (f32[32,18,1]{2,0,1:T(8,128)S(1)}, f32[32,18,1]{2,0,1:T(8,128)S(1)}, u32[]{:S(2)}, u32[]{:S(2)}) collective-permute-start(f32[32,18,1]{2,0,1:T(8,128)S(1)} %get-tuple-element.42), channel_id=1, source_target_pairs={{0,2},{2,4},{4,6},{1,3},{3,5},{5,7},{8,10},{10,12},{12,14},{9,11},... | collective-permute-start | bytes 6920 | tf_op jit(solution)/shard_map/ppermute | solution.py:16
  198.9 5.6 %collective-permute-done.8 = f32[32,18,1]{2,0,1:T(8,128)S(1)} collective-permute-done((f32[32,18,1]{2,0,1:T(8,128)S(1)}, f32[32,18,1]{2,0,1:T(8,128)S(1)}, u32[]{:S(2)}, u32[]{:S(2)}) %collective-permute-start.8) | collective-permute-done | bytes 2336 | tf_op jit(solution)/shard_map/ppermute | solution.py:19
  204.5 1.7 collective-permute-done.9
  208.3 3.0 collective-permute-start.11
  211.4 18.2 %pad_maximum_fusion = f32[2,3,3,34,18,130]{5,3,4,2,1,0:T(8,128)} fusion(f32[2,3,3,1,18,130]{5,3,4,2,1,0:T(1,128)S(1)} %collective-permute-done.5, f32[2,3,3,32,18,1]{5,3,4,2,1,0:T(8,128)S(1)} %copy-done.2, f32[2,3,3,32,1,128]{5,3,4,2,1,0:T(8,128)} %collective-permute-done.1, f32[1,3,3,32,16,128]{5,3,4,2,1,0:T(8,128)S(1)} %copy-done.1, ...), kind=kLoop, calls=%fused_computation.1 | loop fusion | flops 10024560 | bytes 11456640 | tf_op jit(solution)/shard_map/concatenate | solution.py:20
  229.6 9.0 %slice_bitcast_fusion.1 = (f32[3,34,18,130]{3,1,2,0:T(8,128)S(1)}, f32[3,34,18,130]{3,1,2,0:T(8,128)}, f32[3,34,18,130]{3,1,2,0:T(8,128)}, f32[3,34,18,130]{3,1,...) fusion(f32[2,3,3,34,18,130]{5,3,4,2,1,0:T(8,128)} %pad_maximum_fusion), kind=kLoop, calls=%fused_computation.6 | loop fusion | bytes 11456640 | tf_op jit(solution)/shard_map/squeeze | solution.py:77
  238.7 3.1 fusion.47
  243.0 4.5 %collective-permute-start.13 = (f32[32,1,128]{2,0,1:T(8,128)S(1)}, f32[32,1,128]{2,0,1:T(8,128)S(1)}, u32[]{:S(2)}, u32[]{:S(2)}) collective-permute-start(f32[32,1,128]{2,0,1:T(8,128)S(1)} %get-tuple-element.46), channel_id=1, source_target_pairs={{0,8},{8,16},{16,24},{1,9},{9,17},{17,25},{2,10},{10,18},{18,26},{... | collective-permute-start | bytes 49160 | tf_op jit(solution)/shard_map/ppermute | solution.py:16
  247.6 1.4 collective-permute-done.13
  250.5 5.0 %collective-permute-start.15 = (f32[32,18,1]{2,0,1:T(8,128)S(1)}, f32[32,18,1]{2,0,1:T(8,128)S(1)}, u32[]{:S(2)}, u32[]{:S(2)}) collective-permute-start(f32[32,18,1]{2,0,1:T(8,128)S(1)} %get-tuple-element.40), channel_id=1, source_target_pairs={{0,2},{2,4},{4,6},{1,3},{3,5},{5,7},{8,10},{10,12},{12,14},{9,11},... | collective-permute-start | bytes 6920 | tf_op jit(solution)/shard_map/ppermute | solution.py:16
  255.5 3.5 %collective-permute-done.14 = f32[32,18,1]{2,0,1:T(8,128)S(1)} collective-permute-done((f32[32,18,1]{2,0,1:T(8,128)S(1)}, f32[32,18,1]{2,0,1:T(8,128)S(1)}, u32[]{:S(2)}, u32[]{:S(2)}) %collective-permute-start.14) | collective-permute-done | bytes 2336 | tf_op jit(solution)/shard_map/ppermute | solution.py:19
  261.7 3.0 collective-permute-start.17
  265.5 2.8 fusion.35
  269.7 4.5 %collective-permute-start.19 = (f32[32,1,128]{2,0,1:T(8,128)S(1)}, f32[32,1,128]{2,0,1:T(8,128)S(1)}, u32[]{:S(2)}, u32[]{:S(2)}) collective-permute-start(f32[32,1,128]{2,0,1:T(8,128)S(1)} %get-tuple-element.44), channel_id=1, source_target_pairs={{0,8},{8,16},{16,24},{1,9},{9,17},{17,25},{2,10},{10,18},{18,26},{... | collective-permute-start | bytes 49160 | tf_op jit(solution)/shard_map/ppermute | solution.py:16
  274.2 1.4 collective-permute-done.19
  275.8 1.3 collective-permute-start.20
  277.1 5.0 %collective-permute-start.21 = (f32[32,18,1]{2,0,1:T(8,128)S(1)}, f32[32,18,1]{2,0,1:T(8,128)S(1)}, u32[]{:S(2)}, u32[]{:S(2)}) collective-permute-start(f32[32,18,1]{2,0,1:T(8,128)S(1)} %get-tuple-element.38), channel_id=1, source_target_pairs={{0,2},{2,4},{4,6},{1,3},{3,5},{5,7},{8,10},{10,12},{12,14},{9,11},... | collective-permute-start | bytes 6920 | tf_op jit(solution)/shard_map/ppermute | solution.py:16
  282.2 4.7 %collective-permute-done.20 = f32[32,18,1]{2,0,1:T(8,128)S(1)} collective-permute-done((f32[32,18,1]{2,0,1:T(8,128)S(1)}, f32[32,18,1]{2,0,1:T(8,128)S(1)}, u32[]{:S(2)}, u32[]{:S(2)}) %collective-permute-start.20) | collective-permute-done | bytes 2336 | tf_op jit(solution)/shard_map/ppermute | solution.py:19
  289.5 3.2 collective-permute-start.23
  293.4 2.9 fusion.61
  296.2 6.2 %all-to-all-start = ((f32[32,16,128]{2,0,1:T(8,128)}), f32[32,16,128]{2,0,1:T(8,128)S(1)}, u32[]{:S(2)}, u32[]{:S(2)}) async-start(f32[32,16,128]{2,0,1:T(8,128)} %get-tuple-element.8), calls=%async_computation | async-start | bytes 524288 | tf_op jit(solution)/shard_map/all_to_all | solution.py:80
  302.5 9.4 %all-to-all-done = f32[32,16,128]{2,0,1:T(8,128)S(1)} async-done(((f32[32,16,128]{2,0,1:T(8,128)}), f32[32,16,128]{2,0,1:T(8,128)S(1)}, u32[]{:S(2)}, u32[]{:S(2)}) %all-to-all-start) | async-done | bytes 262176 | tf_op jit(solution)/shard_map/all_to_all | solution.py:80
  312.2 1.8 fusion.1
  314.0 6.3 %all-to-all-start.1 = ((f32[16,32,128]{2,1,0:T(8,128)}), f32[16,32,128]{2,1,0:T(8,128)S(1)}, u32[]{:S(2)}, u32[]{:S(2)}) async-start(f32[16,32,128]{2,1,0:T(8,128)} %fusion.1), calls=%async_computation.1 | async-start | bytes 524288 | tf_op jit(solution)/shard_map/all_to_all | solution.py:92
  321.2 9.0 %all-to-all-done.1 = f32[16,32,128]{2,1,0:T(8,128)S(1)} async-done(((f32[16,32,128]{2,1,0:T(8,128)}), f32[16,32,128]{2,1,0:T(8,128)S(1)}, u32[]{:S(2)}, u32[]{:S(2)}) %all-to-all-start.1) | async-done | bytes 262176 | tf_op jit(solution)/shard_map/all_to_all | solution.py:92
  330.4 3.9 %all_to_all.44 = f32[2,16,2048]{2,1,0:T(8,128)S(1)} all-to-all(f32[2,16,2048]{2,1,0:T(8,128)S(1)} %all_to_all.38), channel_id=1, replica_groups=mesh['gx'=4,'gy'=4,'gz'=2] {'gz'}, dimensions={0} | all-to-all | bytes 524288 | tf_op jit(solution)/shard_map/all_to_all | solution.py:91
  335.0 1.9 copy.85
  338.5 1.4 convolution_bitcast_fusion
  (84 shorter events, 24.3 us)
Async XLA Ops:
  0.6 2.8 copy-start.6
  4.4 1.7 copy-start
  4.4 8.6 %copy-start.11 = (u32[32]{0:T(128)S(1)}, u32[32]{0:T(128)}, u32[]{:S(2)}) copy-start(u32[32]{0:T(128)} %constant.97) | copy-start | bytes 388
  4.4 9.8 %copy-start.9 = (s32[96,1]{0,1:T(1,128)S(1)}, s32[96,1]{0,1:T(1,128)}, u32[]{:S(2)}) copy-start(s32[96,1]{0,1:T(1,128)} %param.7) | copy-start | bytes 1156
  4.4 9.9 %copy-start.10 = (s32[96]{0:T(128)S(1)}, s32[96]{0:T(128)}, u32[]{:S(2)}) copy-start(s32[96]{0:T(128)} %param.8) | copy-start | bytes 1156
  4.5 88.7 %copy-start.8 = (f32[96,32]{0,1:T(8,128)S(1)}, f32[96,32]{0,1:T(8,128)}, u32[]{:S(2)}) copy-start(f32[96,32]{0,1:T(8,128)} %param.6) | copy-start | bytes 36868
  6.1 143.3 %collective-permute-start = (f32[2,3,3,32,1,128]{5,3,4,2,1,0:T(8,128)}, f32[2,3,3,32,1,128]{5,3,4,2,1,0:T(8,128)}, u32[]{:S(2)}, u32[]{:S(2)}) collective-permute-start(f32[2,3,3,32,1,128]{5,3,4,2,1,0:T(8,128)} %get-tuple-element.22), channel_id=1, source_target_pairs={{0,8},{8,16},{16,24},{1,9},{9,17},{17,25},{2,10},{10,18},{18,26},{... | collective-permute-start | bytes 884744 | tf_op jit(solution)/shard_map/ppermute | solution.py:16
  11.7 137.7 %collective-permute-start.1 = (f32[2,3,3,32,1,128]{5,3,4,2,1,0:T(8,128)}, f32[2,3,3,32,1,128]{5,3,4,2,1,0:T(8,128)}, u32[]{:S(2)}, u32[]{:S(2)}) collective-permute-start(f32[2,3,3,32,1,128]{5,3,4,2,1,0:T(8,128)} %get-tuple-element.23), channel_id=1, source_target_pairs={{8,0},{16,8},{24,16},{9,1},{17,9},{25,17},{10,2},{18,10},{26,18},{... | collective-permute-start | bytes 884744 | tf_op jit(solution)/shard_map/ppermute | solution.py:19
  143.6 29.6 %collective-permute-start.6 = (f32[32,1,128]{2,0,1:T(8,128)S(1)}, f32[32,1,128]{2,0,1:T(8,128)S(1)}, u32[]{:S(2)}, u32[]{:S(2)}) collective-permute-start(f32[32,1,128]{2,0,1:T(8,128)S(1)} %get-tuple-element.49), channel_id=1, source_target_pairs={{8,0},{16,8},{24,16},{9,1},{17,9},{25,17},{10,2},{18,10},{26,18},{... | collective-permute-start | bytes 49160 | tf_op jit(solution)/shard_map/ppermute | solution.py:19
  144.9 28.3 %collective-permute-start.7 = (f32[32,1,128]{2,0,1:T(8,128)S(1)}, f32[32,1,128]{2,0,1:T(8,128)S(1)}, u32[]{:S(2)}, u32[]{:S(2)}) collective-permute-start(f32[32,1,128]{2,0,1:T(8,128)S(1)} %get-tuple-element.48), channel_id=1, source_target_pairs={{0,8},{8,16},{16,24},{1,9},{9,17},{17,25},{2,10},{10,18},{18,26},{... | collective-permute-start | bytes 49160 | tf_op jit(solution)/shard_map/ppermute | solution.py:16
  162.7 11.1 %collective-permute-start.2 = (f32[2,3,3,32,18,1]{3,0,5,4,2,1:T(2,128)}, f32[2,3,3,32,18,1]{3,0,5,4,2,1:T(2,128)}, u32[]{:S(2)}, u32[]{:S(2)}) collective-permute-start(f32[2,3,3,32,18,1]{3,0,5,4,2,1:T(2,128)} %copy.70), channel_id=1, source_target_pairs={{0,2},{2,4},{4,6},{1,3},{3,5},{5,7},{8,10},{10,12},{12,14},{9,11},... | collective-permute-start | bytes 124424 | tf_op jit(solution)/shard_map/ppermute | solution.py:16
  171.6 7.5 %collective-permute-start.3 = (f32[2,3,3,32,18,1]{3,0,5,4,2,1:T(2,128)}, f32[2,3,3,32,18,1]{3,0,5,4,2,1:T(2,128)}, u32[]{:S(2)}, u32[]{:S(2)}) collective-permute-start(f32[2,3,3,32,18,1]{3,0,5,4,2,1:T(2,128)} %copy.71), channel_id=1, source_target_pairs={{2,0},{4,2},{6,4},{3,1},{5,3},{7,5},{10,8},{12,10},{14,12},{11,9},... | collective-permute-start | bytes 124424 | tf_op jit(solution)/shard_map/ppermute | solution.py:19
  183.7 9.2 %copy-start.3 = (f32[32,18,128]{2,0,1:T(8,128)S(1)}, f32[32,18,128]{2,0,1:T(8,128)}, u32[]{:S(2)}) copy-start(f32[32,18,128]{2,0,1:T(8,128)} %pad_maximum_fusion.10) | copy-start | bytes 884740
  183.7 27.7 %copy-start.1 = (f32[1,3,3,32,16,128]{5,3,4,2,1,0:T(8,128)S(1)}, f32[1,3,3,32,16,128]{5,3,4,2,1,0:T(8,128)}, u32[]{:S(2)}) copy-start(f32[1,3,3,32,16,128]{5,3,4,2,1,0:T(8,128)} %copy-done) | copy-start | bytes 7077892
  183.7 27.7 %copy-start.2 = (f32[2,3,3,32,18,1]{5,3,4,2,1,0:T(8,128)S(1)}, f32[2,3,3,32,18,1]{5,3,4,2,1,0:T(8,128)}, u32[]{:S(2)}) copy-start(f32[2,3,3,32,18,1]{5,3,4,2,1,0:T(8,128)} %copy.73) | copy-start | bytes 124420
  190.3 21.1 %collective-permute-start.4 = (f32[2,3,3,1,18,130]{5,3,4,2,1,0:T(1,128)S(1)}, f32[2,3,3,1,18,130]{5,3,4,2,1,0:T(1,128)S(1)}, u32[]{:S(2)}, u32[]{:S(2)}) collective-permute-start(f32[2,3,3,1,18,130]{5,3,4,2,1,0:T(1,128)S(1)} %get-tuple-element.12), channel_id=1, source_target_pairs={{0,1},{2,3},{4,5},{6,7},{8,9},{10,11},{12,13},{14,15},{16,17},{18,... | collective-permute-start | bytes 505448 | tf_op jit(solution)/shard_map/ppermute | solution.py:16
  191.6 19.8 %collective-permute-start.5 = (f32[2,3,3,1,18,130]{5,3,4,2,1,0:T(1,128)S(1)}, f32[2,3,3,1,18,130]{5,3,4,2,1,0:T(1,128)S(1)}, u32[]{:S(2)}, u32[]{:S(2)}) collective-permute-start(f32[2,3,3,1,18,130]{5,3,4,2,1,0:T(1,128)S(1)} %get-tuple-element.13), channel_id=1, source_target_pairs={{1,0},{3,2},{5,4},{7,6},{9,8},{11,10},{13,12},{15,14},{17,16},{19,... | collective-permute-start | bytes 505448 | tf_op jit(solution)/shard_map/ppermute | solution.py:19
  193.0 11.5 %collective-permute-start.8 = (f32[32,18,1]{2,0,1:T(8,128)S(1)}, f32[32,18,1]{2,0,1:T(8,128)S(1)}, u32[]{:S(2)}, u32[]{:S(2)}) collective-permute-start(f32[32,18,1]{2,0,1:T(8,128)S(1)} %get-tuple-element.43), channel_id=1, source_target_pairs={{2,0},{4,2},{6,4},{3,1},{5,3},{7,5},{10,8},{12,10},{14,12},{11,9},... | collective-permute-start | bytes 6920 | tf_op jit(solution)/shard_map/ppermute | solution.py:19
  194.3 11.9 %collective-permute-start.9 = (f32[32,18,1]{2,0,1:T(8,128)S(1)}, f32[32,18,1]{2,0,1:T(8,128)S(1)}, u32[]{:S(2)}, u32[]{:S(2)}) collective-permute-start(f32[32,18,1]{2,0,1:T(8,128)S(1)} %get-tuple-element.42), channel_id=1, source_target_pairs={{0,2},{2,4},{4,6},{1,3},{3,5},{5,7},{8,10},{10,12},{12,14},{9,11},... | collective-permute-start | bytes 6920 | tf_op jit(solution)/shard_map/ppermute | solution.py:16
  204.5 1.7 copy-start.4
  206.3 0.7 copy-start.5
  207.0 31.6 %collective-permute-start.10 = (f32[1,18,130]{2,0,1:T(1,128)S(1)}, f32[1,18,130]{2,0,1:T(1,128)S(1)}, u32[]{:S(2)}, u32[]{:S(2)}) collective-permute-start(f32[1,18,130]{2,0,1:T(1,128)S(1)} %get-tuple-element.30), channel_id=1, source_target_pairs={{1,0},{3,2},{5,4},{7,6},{9,8},{11,10},{13,12},{15,14},{17,16},{19,... | collective-permute-start | bytes 28088 | tf_op jit(solution)/shard_map/ppermute | solution.py:19
  208.3 30.3 %collective-permute-start.11 = (f32[1,18,130]{2,0,1:T(1,128)S(1)}, f32[1,18,130]{2,0,1:T(1,128)S(1)}, u32[]{:S(2)}, u32[]{:S(2)}) collective-permute-start(f32[1,18,130]{2,0,1:T(1,128)S(1)} %get-tuple-element.31), channel_id=1, source_target_pairs={{0,1},{2,3},{4,5},{6,7},{8,9},{10,11},{12,13},{14,15},{16,17},{18,... | collective-permute-start | bytes 28088 | tf_op jit(solution)/shard_map/ppermute | solution.py:16
  241.7 5.9 %collective-permute-start.12 = (f32[32,1,128]{2,0,1:T(8,128)S(1)}, f32[32,1,128]{2,0,1:T(8,128)S(1)}, u32[]{:S(2)}, u32[]{:S(2)}) collective-permute-start(f32[32,1,128]{2,0,1:T(8,128)S(1)} %get-tuple-element.47), channel_id=1, source_target_pairs={{8,0},{16,8},{24,16},{9,1},{17,9},{25,17},{10,2},{18,10},{26,18},{... | collective-permute-start | bytes 49160 | tf_op jit(solution)/shard_map/ppermute | solution.py:19
  243.0 6.0 %collective-permute-start.13 = (f32[32,1,128]{2,0,1:T(8,128)S(1)}, f32[32,1,128]{2,0,1:T(8,128)S(1)}, u32[]{:S(2)}, u32[]{:S(2)}) collective-permute-start(f32[32,1,128]{2,0,1:T(8,128)S(1)} %get-tuple-element.46), channel_id=1, source_target_pairs={{0,8},{8,16},{16,24},{1,9},{9,17},{17,25},{2,10},{10,18},{18,26},{... | collective-permute-start | bytes 49160 | tf_op jit(solution)/shard_map/ppermute | solution.py:16
  249.2 9.8 %collective-permute-start.14 = (f32[32,18,1]{2,0,1:T(8,128)S(1)}, f32[32,18,1]{2,0,1:T(8,128)S(1)}, u32[]{:S(2)}, u32[]{:S(2)}) collective-permute-start(f32[32,18,1]{2,0,1:T(8,128)S(1)} %get-tuple-element.41), channel_id=1, source_target_pairs={{2,0},{4,2},{6,4},{3,1},{5,3},{7,5},{10,8},{12,10},{14,12},{11,9},... | collective-permute-start | bytes 6920 | tf_op jit(solution)/shard_map/ppermute | solution.py:19
  250.5 9.7 %collective-permute-start.15 = (f32[32,18,1]{2,0,1:T(8,128)S(1)}, f32[32,18,1]{2,0,1:T(8,128)S(1)}, u32[]{:S(2)}, u32[]{:S(2)}) collective-permute-start(f32[32,18,1]{2,0,1:T(8,128)S(1)} %get-tuple-element.40), channel_id=1, source_target_pairs={{0,2},{2,4},{4,6},{1,3},{3,5},{5,7},{8,10},{10,12},{12,14},{9,11},... | collective-permute-start | bytes 6920 | tf_op jit(solution)/shard_map/ppermute | solution.py:16
  260.4 4.3 %collective-permute-start.16 = (f32[1,18,130]{2,0,1:T(1,128)S(1)}, f32[1,18,130]{2,0,1:T(1,128)S(1)}, u32[]{:S(2)}, u32[]{:S(2)}) collective-permute-start(f32[1,18,130]{2,0,1:T(1,128)S(1)} %get-tuple-element.28), channel_id=1, source_target_pairs={{1,0},{3,2},{5,4},{7,6},{9,8},{11,10},{13,12},{15,14},{17,16},{19,... | collective-permute-start | bytes 28088 | tf_op jit(solution)/shard_map/ppermute | solution.py:19
  261.7 3.9 %collective-permute-start.17 = (f32[1,18,130]{2,0,1:T(1,128)S(1)}, f32[1,18,130]{2,0,1:T(1,128)S(1)}, u32[]{:S(2)}, u32[]{:S(2)}) collective-permute-start(f32[1,18,130]{2,0,1:T(1,128)S(1)} %get-tuple-element.29), channel_id=1, source_target_pairs={{0,1},{2,3},{4,5},{6,7},{8,9},{10,11},{12,13},{14,15},{16,17},{18,... | collective-permute-start | bytes 28088 | tf_op jit(solution)/shard_map/ppermute | solution.py:16
  265.5 27.3 %copy-start.7 = (f32[3,32,16,128]{3,2,1,0:T(8,128)S(1)}, f32[3,32,16,128]{3,2,1,0:T(8,128)}, u32[]{:S(2)}) copy-start(f32[3,32,16,128]{3,2,1,0:T(8,128)} %param.11) | copy-start | bytes 2359300
  268.4 5.9 %collective-permute-start.18 = (f32[32,1,128]{2,0,1:T(8,128)S(1)}, f32[32,1,128]{2,0,1:T(8,128)S(1)}, u32[]{:S(2)}, u32[]{:S(2)}) collective-permute-start(f32[32,1,128]{2,0,1:T(8,128)S(1)} %get-tuple-element.45), channel_id=1, source_target_pairs={{8,0},{16,8},{24,16},{9,1},{17,9},{25,17},{10,2},{18,10},{26,18},{... | collective-permute-start | bytes 49160 | tf_op jit(solution)/shard_map/ppermute | solution.py:19
  269.7 6.0 %collective-permute-start.19 = (f32[32,1,128]{2,0,1:T(8,128)S(1)}, f32[32,1,128]{2,0,1:T(8,128)S(1)}, u32[]{:S(2)}, u32[]{:S(2)}) collective-permute-start(f32[32,1,128]{2,0,1:T(8,128)S(1)} %get-tuple-element.44), channel_id=1, source_target_pairs={{0,8},{8,16},{16,24},{1,9},{9,17},{17,25},{2,10},{10,18},{18,26},{... | collective-permute-start | bytes 49160 | tf_op jit(solution)/shard_map/ppermute | solution.py:16
  275.8 11.0 %collective-permute-start.20 = (f32[32,18,1]{2,0,1:T(8,128)S(1)}, f32[32,18,1]{2,0,1:T(8,128)S(1)}, u32[]{:S(2)}, u32[]{:S(2)}) collective-permute-start(f32[32,18,1]{2,0,1:T(8,128)S(1)} %get-tuple-element.39), channel_id=1, source_target_pairs={{2,0},{4,2},{6,4},{3,1},{5,3},{7,5},{10,8},{12,10},{14,12},{11,9},... | collective-permute-start | bytes 6920 | tf_op jit(solution)/shard_map/ppermute | solution.py:19
  277.1 10.9 %collective-permute-start.21 = (f32[32,18,1]{2,0,1:T(8,128)S(1)}, f32[32,18,1]{2,0,1:T(8,128)S(1)}, u32[]{:S(2)}, u32[]{:S(2)}) collective-permute-start(f32[32,18,1]{2,0,1:T(8,128)S(1)} %get-tuple-element.38), channel_id=1, source_target_pairs={{0,2},{2,4},{4,6},{1,3},{3,5},{5,7},{8,10},{10,12},{12,14},{9,11},... | collective-permute-start | bytes 6920 | tf_op jit(solution)/shard_map/ppermute | solution.py:16
  288.2 4.6 %collective-permute-start.22 = (f32[1,18,130]{2,0,1:T(1,128)S(1)}, f32[1,18,130]{2,0,1:T(1,128)S(1)}, u32[]{:S(2)}, u32[]{:S(2)}) collective-permute-start(f32[1,18,130]{2,0,1:T(1,128)S(1)} %get-tuple-element.26), channel_id=1, source_target_pairs={{1,0},{3,2},{5,4},{7,6},{9,8},{11,10},{13,12},{15,14},{17,16},{19,... | collective-permute-start | bytes 28088 | tf_op jit(solution)/shard_map/ppermute | solution.py:19
  289.5 3.9 %collective-permute-start.23 = (f32[1,18,130]{2,0,1:T(1,128)S(1)}, f32[1,18,130]{2,0,1:T(1,128)S(1)}, u32[]{:S(2)}, u32[]{:S(2)}) collective-permute-start(f32[1,18,130]{2,0,1:T(1,128)S(1)} %get-tuple-element.27), channel_id=1, source_target_pairs={{0,1},{2,3},{4,5},{6,7},{8,9},{10,11},{12,13},{14,15},{16,17},{18,... | collective-permute-start | bytes 28088 | tf_op jit(solution)/shard_map/ppermute | solution.py:16
  296.2 15.6 %all-to-all-start = ((f32[32,16,128]{2,0,1:T(8,128)}), f32[32,16,128]{2,0,1:T(8,128)S(1)}, u32[]{:S(2)}, u32[]{:S(2)}) async-start(f32[32,16,128]{2,0,1:T(8,128)} %get-tuple-element.8), calls=%async_computation | async-start | bytes 524288 | tf_op jit(solution)/shard_map/all_to_all | solution.py:80
  314.0 16.2 %all-to-all-start.1 = ((f32[16,32,128]{2,1,0:T(8,128)}), f32[16,32,128]{2,1,0:T(8,128)S(1)}, u32[]{:S(2)}, u32[]{:S(2)}) async-start(f32[16,32,128]{2,1,0:T(8,128)} %fusion.1), calls=%async_computation.1 | async-start | bytes 524288 | tf_op jit(solution)/shard_map/all_to_all | solution.py:92
where the time goes:
time: 341 us; the launch traced here: 340 us
  blocking collectives  120 us (35%)
  starting transfers between devices  77.2 us (23%)
  other arithmetic  52 us (15%)
  local copies, waits for them, and re-layouts  43.3 us (13%)
  waiting for transfers between devices  41.2 us (12%)
  matrix products  4.28 us (1%)
    unnamed x1, blocking collectives  78.5 us
    ppermute x12, starting transfers between devices, with_halo(): lax.ppermute(lax.slice_in_dim(block, block.shape[dim] - width, None, axis...  48.9 us
    all_gather x1, blocking collectives, per_device(): lax.all_gather(well_sources, ('gx', 'gy'), axis=0, tiled=True)  37.5 us
    concatenate x5, other arithmetic, with_halo(): block = jnp.concatenate([low, block, high], axis=dim)  21.7 us
    ppermute x12, starting transfers between devices, with_halo(): lax.ppermute(lax.slice_in_dim(block, 0, width, axis=dim), axis, backward)  15.6 us
    ppermute x12, waiting for transfers between devices, with_halo(): lax.ppermute(lax.slice_in_dim(block, 0, width, axis=dim), axis, backward)  14.6 us
    slice x8, local copies, waits for them, and re-layouts, with_halo(): lax.slice_in_dim(block, block.shape[dim] - width, None, axis=dim)  11.1 us
    scatter-add x1, other arithmetic, per_device(): landed = jnp.zeros((brick_z, columns), jnp.float32).at[:, target].add(jnp...  10.1 us
  transfers between devices with their start and end apart: 26, of which 13 were waited for; matrix products, arithmetic and copies ran while one was open for 19% of the time, Pallas kernels for 0%

commit v1 on v0

v1 whole, which is shorter than its diff:
```python
import functools
import math

import jax
import jax.numpy as jnp
from jax import lax
from jax.experimental import pallas as pl
from jax.experimental.pallas import tpu as pltpu
from jax.sharding import PartitionSpec as P

MESH = pl.DeviceIdType.MESH
LANES = 128
ROWS = 8


def round_up(value, unit):
    return -(-value // unit) * unit


def iota(shape, dim):
    return lax.broadcasted_iota(jnp.int32, shape, dim)


def parts(value):
    high = value.astype(jnp.bfloat16)
    return high, (value - high.astype(jnp.float32)).astype(jnp.bfloat16)


def dot(left, right, dims):
    return lax.dot_general(left, right, (dims, ((), ())), preferred_element_type=jnp.float32)


NN = ((1,), (0,))
NT = ((1,), (1,))
TN = ((0,), (0,))


def flag(mask):
    return jnp.where(mask, 1.0, 0.0).astype(jnp.bfloat16)


def dot_three(left, right, dims):
    left_high, left_low = parts(left)
    right_high, right_low = parts(right)
    return (
        dot(left_high, right_high, dims)
        + dot(left_low, right_high, dims)
        + dot(left_high, right_low, dims)
    )


def kernel(
    sizes, source_ref, owner_ref, cell_ref, flow_any, courant_any, tracer_any,
    lambda_ref, smooth_ref,
    flow_ref, courant_ref, tracer_ref, load_sem,
    payload_ref, well_send, well_recv, well_send_sem, well_recv_sem,
    rise_ref, fall_ref, sum_ref, grad_ref,
    x_send, x_recv, y_send, y_recv, z_send, z_recv, face_send_sem, face_recv_sem,
    carry_send, carry_recv, carry_send_sem, carry_recv_sem,
    bulk_send, bulk_recv, bulk_send_sem, bulk_recv_sem,
    table_high, table_low, wide_ref, stage_ref=None,
):
    n_gx, n_gy, n_gz, brick_z, brick_x, brick_y, cap = sizes
    steps = flow_any.shape[0]
    lines = brick_z * brick_x
    groups = n_gx * n_gy
    devices = groups * n_gz
    a, b, c = lax.axis_index("gx"), lax.axis_index("gy"), lax.axis_index("gz")
    group = a * n_gy + b
    me = group * n_gz + c
    wells = source_ref.shape[1]
    full_z = n_gz * brick_z
    full_x = n_gx * brick_x
    wide_x = round_up(full_x, LANES)
    shares = n_gx * n_gz
    y_rows = brick_y // shares
    pad_rows = round_up(y_rows, ROWS)
    tiles = lines // LANES
    tile_z = LANES // brick_x

    loads = [
        pltpu.make_async_copy(src, dst, load_sem.at[i])
        for i, (src, dst) in enumerate(
            ((courant_any, courant_ref), (flow_any, flow_ref), (tracer_any, tracer_ref))
        )
    ]
    for load in loads:
        load.start()

    for ref in (x_recv, y_recv, z_recv, carry_recv):
        ref[...] = jnp.zeros_like(ref)

    barrier = pltpu.get_barrier_semaphore()

    def greet(d, carried):
        other = lax.rem(me + d, devices)
        pl.semaphore_signal(
            barrier, inc=1,
            device_id=(
                lax.div(other, n_gy * n_gz), lax.rem(lax.div(other, n_gz), n_gy), lax.rem(other, n_gz)
            ),
            device_id_type=MESH,
        )
        return carried

    lax.fori_loop(1, devices, greet, 0)

    eye = iota((wells, wells), 0) == iota((wells, wells), 1)
    before = iota((wells, wells), 0) < iota((wells, wells), 1)
    owner_row = owner_ref[...].astype(jnp.float32)
    owner_col = jnp.sum(jnp.where(eye, owner_row, 0.0), axis=1, keepdims=True)
    rank_row = jnp.sum(
        jnp.where(before & (owner_col == owner_row), 1.0, 0.0), axis=0, keepdims=True
    )
    key_row = (owner_row * cap + rank_row).astype(jnp.int32)
    chosen = flag(iota((groups * cap, wells), 0) == key_row)
    cell_row = cell_ref[...]
    payload_ref[...] = jnp.zeros_like(payload_ref)
    payload_ref[0:brick_z, :] = source_ref[...]
    payload_ref[brick_z:brick_z + 1, :] = lax.div(cell_row, brick_y).astype(jnp.float32)
    payload_ref[brick_z + 1:brick_z + 2, :] = lax.rem(cell_row, brick_y).astype(jnp.float32)
    payload_high, payload_low = parts(payload_ref[...])
    well_send[...] = dot(chosen, payload_high, NT) + dot(chosen, payload_low, NT)

    pl.semaphore_wait(barrier, devices - 1)

    def group_rows(index):
        return pl.ds(pl.multiple_of(index * cap, ROWS), cap)

    def well_copy(d):
        other = lax.rem(group + d, groups)
        return pltpu.make_async_remote_copy(
            src_ref=well_send.at[group_rows(other), :],
            dst_ref=well_recv.at[group_rows(group), :],
            send_sem=well_send_sem.at[d],
            recv_sem=well_recv_sem.at[d],
            device_id=(lax.div(other, n_gy), lax.rem(other, n_gy), c),
            device_id_type=MESH,
        )

    def well_start(d, carried):
        well_copy(d).start()
        return carried

    lax.fori_loop(1, groups, well_start, 0)
    well_recv[group_rows(group), :] = well_send[group_rows(group), :]

    shape = (n_gx * LANES, wide_x)
    at_x = lax.div(iota(shape, 0), LANES) * brick_x + lax.rem(iota(shape, 0), brick_x)
    far = jnp.abs(at_x - iota(shape, 1)).astype(jnp.float32)
    table = jnp.exp(far * (-0.5 / brick_x)) / math.sqrt(2 * brick_x) / math.sqrt(2 * brick_z)
    table = jnp.where(iota(shape, 1) < full_x, table, 0.0)
    depth_of = lax.rem(lax.div(iota(shape, 0), brick_x), tile_z)
    for depth in range(tile_z):
        high, low = parts(jnp.where(depth_of == depth, table, 0.0))
        table_high[:, depth * wide_x:(depth + 1) * wide_x] = high
        table_low[:, depth * wide_x:(depth + 1) * wide_x] = low

    slots = groups * cap
    spread = flag(lax.div(iota((lines, LANES), 0), brick_x) == iota((lines, LANES), 1))
    x_pick = flag(iota((ROWS, LANES), 1) == brick_z)

    loads[0].wait()
    loads[1].wait()
    loads[2].wait()

    def well_wait(d, carried):
        copy = well_copy(d)
        copy.wait_send()
        copy.wait_recv()
        return carried

    lax.fori_loop(1, groups, well_wait, 0)
    landed = well_recv[...]
    landed_high, landed_low = parts(landed)
    x_row = dot(x_pick, landed_high, NT)[0:1, :].astype(jnp.int32)
    x_hit = lax.rem(iota((lines, slots), 0), brick_x) == x_row
    y_hit = flag(
        iota((slots, LANES), 1) == landed[:, brick_z + 1:brick_z + 2].astype(jnp.int32)
    )
    spread_high = jnp.where(x_hit, dot(spread, landed_high, NT), 0.0).astype(jnp.bfloat16)
    spread_low = jnp.where(x_hit, dot(spread, landed_low, NT), 0.0).astype(jnp.bfloat16)
    adjoint = dot(spread_high, y_hit, NN) + dot(spread_low, y_hit, NN)

    y_pos = iota((lines, brick_y), 1)
    x_pos = lax.rem(iota((lines, brick_y), 0), brick_x)
    take_row, take_lane = iota((2 * ROWS, brick_y), 0), iota((2 * ROWS, brick_y), 1)
    take = flag(
        ((take_row < ROWS) & (take_lane == 0)) | ((take_row >= ROWS) & (take_lane == brick_y - 1))
    )
    put = flag(
        ((take_row == 0) & (take_lane == brick_y - 1)) | ((take_row == ROWS) & (take_lane == 0))
    )

    def face_copies(step):
        copies = []
        for axis, (place, count, send, recv) in enumerate(
            ((a, n_gx, x_send, x_recv), (b, n_gy, y_send, y_recv), (c, n_gz, z_send, z_recv))
        ):
            for side in range(2):
                moved = place - 1 if side == 0 else place + 1
                target = [a, b, c]
                target[axis] = lax.rem(moved + count, count)
                sends = place > 0 if side == 0 else place < count - 1
                gets = place < count - 1 if side == 0 else place > 0
                copy = pltpu.make_async_remote_copy(
                    src_ref=send.at[step, side],
                    dst_ref=recv.at[step, side],
                    send_sem=face_send_sem.at[step, axis, side],
                    recv_sem=face_recv_sem.at[step, axis, side],
                    device_id=tuple(target),
                    device_id_type=MESH,
                )
                copies.append((copy, sends, gets))
        return copies

    def when_start(copy, sends):
        @pl.when(sends)
        def _():
            copy.start()

    all_copies = []
    for step in reversed(range(steps)):
        copies = face_copies(step)
        all_copies.extend(copies)
        flow = flow_ref[step]
        flows = [courant_ref[axis] * adjoint for axis in range(3)]
        rise = [
            jnp.where((flow & (1 << axis)) != 0, flows[axis], 0.0) for axis in range(3)
        ]
        fall = [flows[axis] - rise[axis] for axis in range(3)]
        edge = jnp.where(y_pos == 0, rise[1], jnp.where(y_pos == brick_y - 1, fall[1], 0.0))
        edge_high, edge_low = parts(edge)
        edge_rows = dot(take, edge_high, NT) + dot(take, edge_low, NT)
        y_send[step, 0] = edge_rows[0:ROWS]
        y_send[step, 1] = edge_rows[ROWS:2 * ROWS]
        when_start(*copies[2][:2])
        when_start(*copies[3][:2])
        rise_ref[...] = rise[0]
        fall_ref[...] = fall[0]
        x_send[step, 0] = rise_ref[pl.ds(0, brick_z, stride=brick_x), :]
        x_send[step, 1] = fall_ref[pl.ds(brick_x - 1, brick_z, stride=brick_x), :]
        when_start(*copies[0][:2])
        when_start(*copies[1][:2])
        z_send[step, 0] = rise[2][0:brick_x]
        z_send[step, 1] = fall[2][lines - brick_x:lines]
        when_start(*copies[4][:2])
        when_start(*copies[5][:2])

        rest = 1.0 - (courant_ref[0] + courant_ref[1] + courant_ref[2])
        updated = rest * adjoint
        updated = updated + jnp.where(
            x_pos == brick_x - 1, 0.0, pltpu.roll(rise[0], lines - 1, 0)
        )
        updated = updated + jnp.where(x_pos == 0, 0.0, pltpu.roll(fall[0], 1, 0))
        updated = updated + jnp.where(
            y_pos == brick_y - 1, 0.0, pltpu.roll(rise[1], brick_y - 1, 1)
        )
        updated = updated + jnp.where(y_pos == 0, 0.0, pltpu.roll(fall[1], 1, 1))
        border = jnp.zeros((brick_x, brick_y), jnp.float32)
        updated = updated + jnp.concatenate([rise[2][brick_x:], border], axis=0)
        updated = updated + jnp.concatenate([border, fall[2][:lines - brick_x]], axis=0)
        sum_ref[...] = updated

        for copy, _, gets in copies:
            @pl.when(gets)
            def _():
                copy.wait_recv()

        top = pl.ds(brick_x - 1, brick_z, stride=brick_x)
        bottom = pl.ds(0, brick_z, stride=brick_x)
        sum_ref[top, :] = sum_ref[top, :] + x_recv[step, 0]
        sum_ref[bottom, :] = sum_ref[bottom, :] + x_recv[step, 1]
        last = pl.ds(lines - brick_x, brick_x)
        sum_ref[last, :] = sum_ref[last, :] + z_recv[step, 0]
        first = pl.ds(0, brick_x)
        sum_ref[first, :] = sum_ref[first, :] + z_recv[step, 1]
        side_rows = jnp.concatenate([y_recv[step, 0], y_recv[step, 1]], axis=0)
        side_high, side_low = parts(side_rows)
        adjoint = sum_ref[...] + (dot(side_high, put, TN) + dot(side_low, put, TN))
        if step == steps - 1:
            gradient = adjoint * tracer_ref[step]
        else:
            gradient = grad_ref[...] + adjoint * tracer_ref[step]
        grad_ref[...] = gradient

    length = 2.0 * brick_y
    from_end = jnp.where(take_row < ROWS, brick_y - take_lane, take_lane + 1)
    pull = jnp.exp(from_end.astype(jnp.float32) * (-1.0 / length)) / math.sqrt(length)
    carries = dot_three(pull, gradient, NT)
    carry_send[0] = carries[0:ROWS]
    carry_send[1] = carries[ROWS:2 * ROWS]
    carry_copies = []
    for d in range(1, n_gy):
        for side in range(2):
            moved = b + d if side == 0 else b - d
            back = b - d if side == 0 else b + d
            copy = pltpu.make_async_remote_copy(
                src_ref=carry_send.at[side],
                dst_ref=carry_recv.at[pl.ds(pl.multiple_of(b * ROWS, ROWS), ROWS), :],
                send_sem=carry_send_sem.at[side, d],
                recv_sem=carry_recv_sem.at[side, d],
                device_id=(a, lax.rem(moved + n_gy, n_gy), c),
                device_id_type=MESH,
            )
            sends = (moved >= 0) & (moved < n_gy)
            gets = (back >= 0) & (back < n_gy)
            when_start(copy, sends)
            carry_copies.append((copy, sends, gets))

    lambda_ref[...] = adjoint

    def line_place(row):
        return lax.div(row, pad_rows) * y_rows + lax.rem(row, pad_rows)

    shape = (shares * pad_rows, brick_y)
    near = jnp.abs(line_place(iota(shape, 0)) - iota(shape, 1)).astype(jnp.float32)
    table_y = jnp.exp(near * (-1.0 / length)) / math.sqrt(length)
    local = dot_three(table_y, gradient, NT)

    shape = (shares * pad_rows, n_gy * ROWS)
    at_y = line_place(iota(shape, 0))
    brick = lax.div(iota(shape, 1), ROWS)
    gap = jnp.where(
        brick < b,
        at_y + brick_y * (b - brick - 1),
        brick_y - 1 - at_y + brick_y * (brick - b - 1),
    )
    useful = (lax.rem(iota(shape, 1), ROWS) == 0) & (brick != b)
    gap = jnp.where(useful, gap, 0)
    push = jnp.where(useful, jnp.exp(gap.astype(jnp.float32) * (-1.0 / length)), 0.0)

    for copy, _, gets in carry_copies:
        @pl.when(gets)
        def _():
            copy.wait_recv()

    bulk_send[...] = local + dot_three(push, carry_recv[...], NN)

    mine = a * n_gz + c

    def bulk_copy(d):
        share = lax.rem(mine + d, shares)
        other = b * shares + share
        return other, pltpu.make_async_remote_copy(
            src_ref=bulk_send.at[pl.ds(pl.multiple_of(share * pad_rows, ROWS), pad_rows), :],
            dst_ref=bulk_recv.at[mine],
            send_sem=bulk_send_sem.at[share],
            recv_sem=bulk_recv_sem.at[mine],
            device_id=(
                lax.div(other, n_gy * n_gz), lax.rem(lax.div(other, n_gz), n_gy), lax.rem(other, n_gz)
            ),
            device_id_type=MESH,
        )

    def bulk_start(d, carried):
        other, copy = bulk_copy(d)

        @pl.when(other != me)
        def _():
            copy.start()

        return carried

    lax.fori_loop(0, shares, bulk_start, 0)

    own = lax.div(me, shares) == b

    @pl.when(own)
    def _():
        rows = pl.ds(pl.multiple_of((me - b * shares) * pad_rows, ROWS), pad_rows)
        bulk_recv[mine] = bulk_send[rows, :]

    for copy, sends, _ in all_copies + carry_copies:
        @pl.when(sends)
        def _():
            copy.wait_send()

    def bulk_wait(d, carried):
        share = lax.rem(mine + d, shares)

        @pl.when(jnp.logical_not(own & (share == mine)))
        def _():
            pltpu.make_async_remote_copy(
                src_ref=bulk_send.at[pl.ds(0, pad_rows), :],
                dst_ref=bulk_recv.at[share],
                send_sem=bulk_send_sem.at[share],
                recv_sem=bulk_recv_sem.at[share],
                device_id=(a, b, c),
                device_id_type=MESH,
            ).wait_recv()

        return carried

    lax.fori_loop(0, shares, bulk_wait, 0)

    rows = [
        jnp.concatenate(
            [
                bulk_recv[i * n_gz + k, :, t * LANES:(t + 1) * LANES]
                for i in range(n_gx)
            ],
            axis=1,
        )
        for k in range(n_gz)
        for t in range(tiles)
    ]
    high, low = parts(jnp.concatenate(rows, axis=0))
    wide_ref[...] = (
        dot(high, table_high[...], NN)
        + dot(low, table_high[...], NN)
        + dot(high, table_low[...], NN)
    )

    fade = math.exp(-0.5 / brick_z)

    def plane(z):
        row, depth = z // tile_z * pad_rows, z % tile_z
        return wide_ref[row:row + y_rows, depth * wide_x:(depth + 1) * wide_x]

    ahead = [plane(0)]
    for z in range(1, full_z):
        ahead.append(plane(z) + fade * ahead[-1])
    behind = None
    for z in reversed(range(full_z)):
        total = ahead[z] if behind is None else ahead[z] + behind
        if full_x <= LANES:
            smooth_ref[pl.ds(z, y_rows, stride=full_z), :] = total[:, 0:full_x]
        else:
            for tile in range(wide_x // LANES):
                part = total[:, tile * LANES:(tile + 1) * LANES]
                stage_ref[tile, pl.ds(z, y_rows, stride=full_z), :] = part
        behind = fade * (plane(z) if behind is None else plane(z) + behind)

    if full_x > LANES:
        for tile in range(wide_x // LANES):
            end = min((tile + 1) * LANES, full_x)
            smooth_ref[:, tile * LANES:end] = stage_ref[tile][:, 0:end - tile * LANES]

    def bulk_sent(d, carried):
        other, copy = bulk_copy(d)

        @pl.when(other != me)
        def _():
            copy.wait_send()

        return carried

    lax.fori_loop(0, shares, bulk_sent, 0)


def per_device(well_sources, well_owner, well_cell, flow_sign, courant, tracer):
    steps, brick_z, brick_x, brick_y = tracer.shape
    n_gx, n_gy, n_gz = lax.axis_size("gx"), lax.axis_size("gy"), lax.axis_size("gz")
    groups, shares = n_gx * n_gy, n_gx * n_gz
    wells = well_cell.shape[0]
    cap = round_up(2 * -(-wells // groups), ROWS)
    lines = brick_z * brick_x
    y_rows = brick_y // shares
    pad_rows = round_up(y_rows, ROWS)
    full_x, full_z = n_gx * brick_x, n_gz * brick_z
    wide_x = round_up(full_x, LANES)
    tile_z = LANES // brick_x
    tiles = lines // LANES
    f32 = jnp.float32
    sizes = (n_gx, n_gy, n_gz, brick_z, brick_x, brick_y, cap)
    dma = pltpu.SemaphoreType.DMA
    vmem = pl.BlockSpec(memory_space=pltpu.VMEM)
    away = pl.BlockSpec(memory_space=pl.ANY)
    field = (3, lines, brick_y)
    stage = []
    if full_x > LANES:
        stage = [pltpu.VMEM((wide_x // LANES, y_rows * full_z, LANES), f32)]
    run = pl.pallas_call(
        functools.partial(kernel, sizes),
        out_shape=(
            jax.ShapeDtypeStruct((lines, brick_y), f32),
            jax.ShapeDtypeStruct((y_rows * full_z, full_x), f32),
        ),
        in_specs=[vmem, vmem, vmem, away, away, away],
        out_specs=(vmem, vmem),
        scratch_shapes=[
            pltpu.VMEM((steps, lines, brick_y), jnp.int32),
            pltpu.VMEM(field, f32),
            pltpu.VMEM((steps, lines, brick_y), f32),
            dma((3,)),
            pltpu.VMEM((LANES, wells), f32),
            pltpu.VMEM((groups * cap, LANES), f32),
            pltpu.VMEM((groups * cap, LANES), f32),
            dma((groups,)),
            dma((groups,)),
            pltpu.VMEM((lines, brick_y), f32),
            pltpu.VMEM((lines, brick_y), f32),
            pltpu.VMEM((lines, brick_y), f32),
            pltpu.VMEM((lines, brick_y), f32),
            pltpu.VMEM((steps, 2, brick_z, brick_y), f32),
            pltpu.VMEM((steps, 2, brick_z, brick_y), f32),
            pltpu.VMEM((steps, 2, ROWS, lines), f32),
            pltpu.VMEM((steps, 2, ROWS, lines), f32),
            pltpu.VMEM((steps, 2, brick_x, brick_y), f32),
            pltpu.VMEM((steps, 2, brick_x, brick_y), f32),
            dma((steps, 3, 2)),
            dma((steps, 3, 2)),
            pltpu.VMEM((2, ROWS, lines), f32),
            pltpu.VMEM((n_gy * ROWS, lines), f32),
            dma((2, n_gy)),
            dma((2, n_gy)),
            pltpu.VMEM((shares * pad_rows, lines), f32),
            pltpu.VMEM((shares, pad_rows, lines), f32),
            dma((shares,)),
            dma((shares,)),
            pltpu.VMEM((n_gx * LANES, tile_z * wide_x), jnp.bfloat16),
            pltpu.VMEM((n_gx * LANES, tile_z * wide_x), jnp.bfloat16),
            pltpu.VMEM((n_gz * tiles * pad_rows, tile_z * wide_x), f32),
        ] + stage,
        compiler_params=pltpu.CompilerParams(
            collective_id=0, has_side_effects=True, vmem_limit_bytes=56 * 2**20
        ),
    )
    start, smoothed = run(
        well_sources.T,
        well_owner.reshape(1, wells),
        well_cell.reshape(1, wells),
        flow_sign.reshape(steps, lines, brick_y),
        courant.reshape(field),
        tracer.reshape(steps, lines, brick_y),
    )
    return (
        start.reshape(brick_z, brick_x, brick_y),
        smoothed.reshape(y_rows, full_z, full_x),
    )


def solution(mesh):
    return jax.shard_map(
        per_device,
        mesh=mesh,
        in_specs=(
            P(("gx", "gy"), "gz"),
            P(("gx", "gy"), None),
            P(("gx", "gy")),
            P(None, "gz", "gx", "gy"),
            P(None, "gz", "gx", "gy"),
            P(None, "gz", "gx", "gy"),
        ),
        out_specs=(P("gz", "gx", "gy"), P(("gx", "gy", "gz"), None, None)),
        check_vma=False,
    )
```

time: 341 us -> 41.1 us (0.12)
  blocking collectives: 120 us -> 0 us
  starting transfers between devices: 77.2 us -> 0 us
  other arithmetic: 52 us -> 0 us
  waiting for transfers between devices: 41.2 us -> 0 us
  local copies, waits for them, and re-layouts: 43.3 us -> 2.52 us
  Pallas kernels: 0 us -> 37.7 us
  matrix products: 4.28 us -> 0 us
    unnamed x1 -> x0, blocking collectives: 78.5 us -> none
    ppermute x24 -> x0, starting transfers between devices: 64.6 us -> none  [the longest x12 48.9 us: with_halo(): lax.ppermute(lax.slice_in_dim(block, block.shape[dim] - width, None, axis...]
    pallas_call x0 -> x1, Pallas kernels: none -> 37.7 us  [per_device(): run(well_sources.T, well_owner.reshape(1, wells), well_cell.reshape(1, we...]
    all_gather x1 -> x0, blocking collectives: 37.5 us -> none  [per_device(): lax.all_gather(well_sources, ('gx', 'gy'), axis=0, tiled=True)]
    ppermute x24 -> x0, waiting for transfers between devices: 22.9 us -> none  [the longest x12 14.6 us: with_halo(): lax.ppermute(lax.slice_in_dim(block, 0, width, axis=dim), axis, backward)]
    concatenate x5 -> x0, other arithmetic: 21.7 us -> none  [with_halo(): block = jnp.concatenate([low, block, high], axis=dim)]
    all_to_all x2 -> x0, waiting for transfers between devices: 18.3 us -> none  [the longest x1 9.37 us: per_device(): lax.all_to_all(gradient, 'gy', split_axis=1, concat_axis=2, tiled=True)]
    slice x10 -> x0, local copies, waits for them, and re-layouts: 15.5 us -> none  [the longest x8 11.1 us: with_halo(): lax.slice_in_dim(block, block.shape[dim] - width, None, axis=dim)]
  transfers between devices with their start and end apart: 26 -> 0, of which waited for: 13 -> 0; matrix products, arithmetic and copies ran while one was open for 19% -> 0% of each run, Pallas kernels for 0% -> 0%
where the time goes in v1:
time: 41.1 us; the launch traced here: 40.9 us
  Pallas kernels  37.7 us (92%)
  local copies, waits for them, and re-layouts  2.52 us (6%)
  between operations  0.65 us (2%)
    pallas_call x1, Pallas kernels, per_device(): run(well_sources.T, well_owner.reshape(1, wells), well_cell.reshape(1, we...  37.7 us
    unnamed x4, local copies, waits for them, and re-layouts  2.52 us

profile of v1, /device:TPU:0, one launch (start us, length us, event | category | flops | bytes accessed | tf_op | source)
XLA Modules:
  0.0 40.9 jit_solution(2254080783973151877)
XLA Ops:
  0.6 37.7 %shard_map.77 = (f32[512,128]{1,0:T(8,128)}, f32[1024,64]{1,0:T(8,128)}) custom-call(f32[32,96]{1,0:T(8,128)} %bitcast.13, s32[1,96]{1,0:T(1,128)} %bitcast.14, s32[1,96]{1,0:T(1,128)} %bitcast.15, s32[3,512,128]{2,1,0:T(8,128)} %bitcast.8, f32[3,512,128]{2,1,0:T(8,128)} %bitcast.9, f32[3,512,128]{2,1,0:T(8,128)} %bitcast.10), custom_call_target="tpu_custom_call" | custom-call | tf_op jit(solution)/shard_map/pallas_call | solution.py:520
  38.3 0.0 copy-start
  38.3 1.7 %copy.10 = f32[32,16,128]{2,1,0:T(8,128)} copy(f32[32,16,128]{2,1,0:T(8,128)} %bitcast.12) | data formatting | bytes 524288
  40.1 0.0 copy-done
  40.1 0.8 %copy.11 = f32[16,64,64]{2,1,0:T(8,128)} copy(f32[16,64,64]{2,1,0:T(8,128)S(1)} %bitcast.11) | data formatting | bytes 524288
Async XLA Ops:
  38.3 1.7 %copy-start = (f32[1024,64]{1,0:T(8,128)S(1)}, f32[1024,64]{1,0:T(8,128)}, u32[]{:S(2)}) copy-start(f32[1024,64]{1,0:T(8,128)} %get-tuple-element.5) | copy-start | bytes 786436
